TPU v7x, 512 devices: a whole 4x8x8 slice. The times are simulated.
512 devices in a mesh: sib: 2 (over core), row: 16 (over z, y_lo), col: 16 (over x, y_hi).
Axes of the slice: x: 4, y: 8 (y_hi: 4, y_lo: 2; y = y_hi * 2 + y_lo), z: 8, core: 2. Of those that a mesh axis runs over, the one named last changes fastest.
Arguments:
- child_front: float32 [2, 8192, 8192], P('sib', 'row', 'col'), may hold values from -6 to 6
- child_panel: float32 [2, 8192, 1024], P('sib', ('row', 'col')), may hold values from -0.42 to 0.42
- block_map: int32 [2, 64], replicated, may hold values from 0 to 95, as said below
- parent_front: float32 [12288, 12288], P(('row', 'sib'), 'col'), may hold values from -6 to 6
- pivot_inverse: float32 [512, 512], replicated, may hold values from -0.03 to 0.1, as said below
Outputs:
- parent_out: float32 [12288, 12288], P(('row', 'sib'), 'col')
Inputs may be any that keep to these rules, and one draw needn't show every extreme that they name: `block_map`: each row is strictly increasing. A child block i that lands in parent block g * 6 + k with 0 <= k < 6 satisfies g * 4 - 2 <= i < (g + 1) * 4; the lower end is met for g = 1 in every draw, and the last parent block is always named. `pivot_inverse`: lower triangular with diagonal entries from 0.05 to 0.1.
All inputs are finite; a program needn't handle non-finite values.
Results may differ from a plain program's by a relative error of at most 0.0001.
Values sent between devices are 32-bit elements; how exact they have to be, the bound alone decides.
A program may use at most 64 MiB of HBM per device.

v0:
```python
import jax
import jax.numpy as jnp
from jax import lax
from jax.sharding import Mesh
from jax.sharding import PartitionSpec as P

BLK = 128
CBD = 4
PBD = 6
HB = 2
PANEL = 512
ROW = ("row_0", "row_1")
ROW_COL = ("row_0", "row_1", "col")
ROW_SIB = ("row_0", "row_1", "sib")


def broadcast_by_axis(value, axes, root):
    value = jnp.where(lax.axis_index(axes) == root, value, jnp.zeros_like(value))
    for axis in axes:
        value = lax.psum(value, axis)
    return value


def shifted(value, axis, steps):
    count = lax.axis_size(axis)
    initial, last = (max(0, -steps), min(count, count - steps))
    return lax.ppermute(value, axis, [(source, source + steps) for source in range(initial, last)])


def split_up(value, dim, devices):
    shape = value.shape
    blocks = value.reshape(*shape[:dim], devices, shape[dim] // devices, *shape[dim + 1 :])
    return jnp.moveaxis(blocks, dim, 0)


def summed_on_arrival(value, axis, dim):
    blocks = split_up(value, dim, lax.axis_size(axis))
    arrived = lax.all_to_all(blocks, axis, split_axis=0, concat_axis=0, tiled=True)
    return arrived.sum(axis=0)


def padded_to(lines, devices):
    spare = -len(lines) % devices
    return jnp.pad(lines, [(0, spare)] + [(0, 0)] * (lines.ndim - 1))


def spread(value, axis, root):
    lines = jnp.where(lax.axis_index(axis) == root, value, jnp.zeros_like(value)).reshape(
        -1, *value.shape[1:][-1:]
    )
    padded = padded_to(lines, lax.axis_size(axis))
    own = lax.psum_scatter(padded, axis, scatter_dimension=0, tiled=True)
    return lax.all_gather(own, axis, axis=0, tiled=True)[: len(lines)].reshape(value.shape)


def from_everyone(value, axis):
    devices = lax.axis_size(axis)
    return lax.all_to_all(
        jnp.broadcast_to(value[None], (devices, *value.shape)), axis, 0, 0, tiled=True
    )


def joined_along(blocks, dim):
    shape = list(blocks.shape[1:])
    shape[dim] *= blocks.shape[0]
    return jnp.moveaxis(blocks, 0, dim).reshape(shape)


def collect(value, axis, dim):
    blocks = from_everyone(value, axis)
    return joined_along(blocks, dim)


def choose_blocks(block_row, device, child_span, parent_span, edge_span):
    padded = jnp.concatenate([jnp.full((edge_span,), -1, jnp.int32), block_row])
    window = lax.dynamic_slice_in_dim(padded, device * child_span, child_span + edge_span)
    target = device * parent_span + jnp.arange(parent_span, dtype=jnp.int32)
    return (window[None, :] == target[:, None]).astype(jnp.float32)


def times_inverse(rows_part, pivot_inverse):
    return lax.dot_general(
        rows_part,
        pivot_inverse,
        (((1,), (1,)), ((), ())),
        precision=lax.Precision.HIGHEST,
        preferred_element_type=jnp.float32,
    )


def shards(child_front, child_panel, block_map, parent_front, pivot_inverse):
    front_index = lax.axis_index("sib")
    row_index = lax.axis_index(ROW)
    col_index = lax.axis_index("col")
    child_rows = child_front.shape[1]
    parent_rows = parent_front.shape[0]
    parent_cols = parent_front.shape[1]
    edge_width = HB * BLK
    span_blocks = CBD + HB
    rows_local = lax.all_gather(child_panel, "col", axis=1, tiled=True)[0]
    cols_local = broadcast_by_axis(rows_local, ROW, col_index)
    update = child_front[0] - lax.dot_general(
        rows_local,
        cols_local,
        (((1,), (1,)), ((), ())),
        precision=lax.Precision.HIGHEST,
        preferred_element_type=jnp.float32,
    )
    my_map = lax.dynamic_index_in_dim(block_map, front_index, 0, keepdims=False)
    left_cols = shifted(update[:, -edge_width:], "col", 1)
    col_window = jnp.concatenate([left_cols, update], axis=1).reshape(child_rows, span_blocks, BLK)
    col_pick = choose_blocks(my_map, col_index, CBD, PBD, HB)
    spread_cols = jnp.einsum(
        "rwk,qw->rqk", col_window, col_pick, precision=lax.Precision.HIGHEST
    ).reshape(child_rows, PBD * BLK)
    left_rows = shifted(spread_cols[-edge_width:], ROW, 1)
    row_window = jnp.concatenate([left_rows, spread_cols], axis=0).reshape(
        span_blocks, BLK, PBD * BLK
    )
    row_pick = choose_blocks(my_map, row_index, CBD, PBD, HB)
    spread_both = jnp.einsum(
        "wtc,qw->qtc", row_window, row_pick, precision=lax.Precision.HIGHEST
    ).reshape(PBD * BLK, PBD * BLK)
    summed = summed_on_arrival(spread_both, "sib", 0)
    assembled = parent_front + summed
    local_factor = times_inverse(assembled[:, :PANEL], pivot_inverse)
    factor_rows = spread(local_factor, "col", 0)
    owner_rows = broadcast_by_axis(factor_rows, ROW, col_index)
    col_factor = collect(owner_rows, "sib", 0)
    product = lax.dot_general(
        factor_rows,
        col_factor,
        (((1,), (1,)), ((), ())),
        precision=lax.Precision.HIGHEST,
        preferred_element_type=jnp.float32,
    )
    global_rows = (row_index * 2 + front_index) * parent_rows + jnp.arange(
        parent_rows, dtype=jnp.int32
    )
    global_cols = col_index * parent_cols + jnp.arange(parent_cols, dtype=jnp.int32)
    inside = (global_rows[:, None] >= PANEL) & (global_cols[None, :] >= PANEL)
    trailing = jnp.where(inside, assembled - product, assembled)
    factor_wide = jnp.pad(factor_rows, ((0, 0), (0, parent_cols - PANEL)))
    return jnp.where(global_cols[None, :] < PANEL, factor_wide, trailing)


def solution(mesh):
    split = Mesh(
        mesh.devices.reshape(mesh.shape["sib"], 8, 2, mesh.shape["col"]),
        ("sib", "row_0", "row_1", "col"),
    )
    placed = (P("sib", ROW, "col"), P("sib", ROW_COL, None), P(), P(ROW_SIB, "col"), P())
    return jax.shard_map(
        shards, mesh=split, in_specs=placed, out_specs=P(ROW_SIB, "col"), check_vma=False
    )
```

profile of v0, /device:TPU:1, one launch (start us, length us, event | category | flops | bytes accessed | tf_op | source)
XLA Modules:
  0.0 621.0 jit_solution(6062125449259001521)
XLA Ops:
  7.3 72.9 %all-gather.2.cloned.1.call-done = f32[1,512,1024]{2,1,0:T(8,128)} async-done(((f32[1,32,1024]{2,1,0:T(8,128)}), f32[1,512,1024]{2,1,0:T(8,128)}) %all-gather.2.cloned.1.call-update) | async-done | bytes 2097168 | tf_op jit(solution)/shard_map/all_gather | solution.py:100
  80.2 3.2 bitcast_select_fusion
  83.4 82.9 %all-reduce.7.cloned.1.call-done = f32[512,1024]{1,0:T(8,128)} async-done(((f32[512,1024]{1,0:T(8,128)}), f32[512,1024]{1,0:T(8,128)}) %all-reduce.7.cloned.1.call-update) | async-done | bytes 2097168 | tf_op jit(solution)/shard_map/psum | solution.py:20
  166.4 2.7 copy.8
  169.1 81.5 %all-reduce.9.cloned.1.call-done = f32[512,1024]{1,0:T(8,128)} async-done(((f32[512,1024]{1,0:T(8,128)}), f32[512,1024]{1,0:T(8,128)}) %all-reduce.9.cloned.1.call-update) | async-done | bytes 2097168 | tf_op jit(solution)/shard_map/psum | solution.py:20
  250.6 5.4 fusion.8
  257.0 4.1 collective-permute-start
  261.2 13.7 %collective-permute-done = f32[512,256]{0,1:T(8,128)S(1)} collective-permute-done((f32[512,256]{0,1:T(8,128)S(1)}, f32[512,256]{0,1:T(8,128)S(1)}, u32[]{:S(2)}, u32[]{:S(2)}) %collective-permute-start) | collective-permute-done | bytes 524320 | tf_op jit(solution)/shard_map/ppermute | solution.py:27
  276.3 1.8 copy.9
  278.2 2.7 convolution_bitcast_fusion
  281.9 2.4 copy.10
  284.3 11.1 %collective-permute-start.1 = (f32[256,768]{0,1:T(8,128)}, f32[256,768]{0,1:T(8,128)}, u32[]{:S(2)}, u32[]{:S(2)}) collective-permute-start(f32[256,768]{0,1:T(8,128)} %bitcast.40), channel_id=1, source_target_pairs={{0,16},{16,32},{32,48},{48,64},{64,80},{80,96},{96,112},{112,128},... | collective-permute-start | bytes 2359304 | tf_op jit(solution)/shard_map/ppermute | solution.py:27
  297.0 13.2 %collective-permute-done.1 = f32[256,768]{0,1:T(8,128)} collective-permute-done((f32[256,768]{0,1:T(8,128)}, f32[256,768]{0,1:T(8,128)}, u32[]{:S(2)}, u32[]{:S(2)}) %collective-permute-start.1) | collective-permute-done | bytes 786464 | tf_op jit(solution)/shard_map/ppermute | solution.py:27
  310.2 3.2 pad_maximum_fusion
  313.4 2.0 copy.12
  315.4 2.9 fusion
  319.1 7.7 %all_to_all.10 = f32[2,384,768]{2,1,0:T(8,128)S(1)} all-to-all(f32[2,384,768]{2,1,0:T(8,128)S(1)} %bitcast.36), channel_id=1, replica_groups=mesh['sib'=2,'row_0'=8,'row_1'=2,'col'=16] {'sib'}, dimensions={0} | all-to-all | bytes 4718592 | tf_op jit(solution)/shard_map/all_to_all | solution.py:38
  329.8 2.3 convolution_select_fusion
  332.2 94.5 %reduce-scatter.2.cloned.1.call-done = f32[24,512]{1,0:T(8,128)} async-done(((f32[384,512]{1,0:T(8,128)}), f32[24,512]{1,0:T(8,128)}) %reduce-scatter.2.cloned.1.call-update) | async-done | bytes 49168 | tf_op jit(solution)/shard_map/reduce_scatter | solution.py:52
  426.7 41.6 %all_gather.7 = f32[384,512]{1,0:T(8,128)S(1)} all-gather(f32[24,512]{1,0:T(8,128)} %reduce-scatter.2.cloned.1.call-done), channel_id=1, replica_groups=mesh['sib'=2,'row_0'=8,'row_1'=2,'col'=16] {'col'}, dimensions={0}, use_global_device_ids=true | all-gather | bytes 835584 | tf_op jit(solution)/shard_map/all_gather | solution.py:53
  469.3 78.7 %all-reduce.11.cloned.1.call-done = f32[384,512]{1,0:T(8,128)} async-done(((f32[384,512]{1,0:T(8,128)}), f32[384,512]{1,0:T(8,128)}) %all-reduce.11.cloned.1.call-update) | async-done | bytes 786448 | tf_op jit(solution)/shard_map/psum | solution.py:20
  548.1 56.2 %all-reduce.13.cloned.1.call-done = f32[384,512]{1,0:T(8,128)} async-done(((f32[384,512]{1,0:T(8,128)}), f32[384,512]{1,0:T(8,128)}) %all-reduce.13.cloned.1.call-update) | async-done | bytes 786448 | tf_op jit(solution)/shard_map/psum | solution.py:20
  605.6 5.3 all_to_all.11
  610.9 3.2 fusion.4
  (35 shorter events, 12.2 us)
Async XLA Ops:
  6.5 323.3 %copy-start = (f32[512,512]{1,0:T(8,128)S(1)}, f32[512,512]{1,0:T(8,128)}, u32[]{:S(2)}) copy-start(f32[512,512]{1,0:T(8,128)} %param.9) | copy-start | bytes 3145732
  6.5 73.6 %all-gather.2.cloned.1.call-start = ((), (), s32[]{:S(2)}) async-start(), calls=%async_computation.3 | async-start | bytes 2228224 | tf_op jit(solution)/shard_map/all_gather | solution.py:100
  7.3 159.1 %all-reduce.7.cloned.1.call-start = ((), (), s32[]{:S(2)}) async-start(), calls=%async_computation.4 | async-start | bytes 4194304 | tf_op jit(solution)/shard_map/psum | solution.py:20
  83.4 167.2 %all-reduce.9.cloned.1.call-start = ((), (), s32[]{:S(2)}) async-start(), calls=%async_computation.5 | async-start | bytes 4194304 | tf_op jit(solution)/shard_map/psum | solution.py:20
  166.4 84.2 %copy-start.1 = (f32[1,512,1024]{2,1,0:T(8,128)S(1)}, f32[1,512,1024]{2,1,0:T(8,128)}, u32[]{:S(2)}) copy-start(f32[1,512,1024]{2,1,0:T(8,128)} %all-gather.2.cloned.1.call-done) | copy-start | bytes 6291460
  166.4 260.3 %reduce-scatter.2.cloned.1.call-start = ((), (), s32[]{:S(2)}) async-start(), calls=%async_computation.6 | async-start | bytes 835584 | tf_op jit(solution)/shard_map/reduce_scatter | solution.py:52
  169.1 92.0 %copy-start.3 = (s32[2,64]{1,0:T(2,128)S(1)}, s32[2,64]{1,0:T(2,128)}, u32[]{:S(2)}) copy-start(s32[2,64]{1,0:T(2,128)} %param.7) | copy-start | bytes 1540
  256.0 1.0 copy-start.2
  257.0 17.9 %collective-permute-start = (f32[512,256]{0,1:T(8,128)S(1)}, f32[512,256]{0,1:T(8,128)S(1)}, u32[]{:S(2)}, u32[]{:S(2)}) collective-permute-start(f32[512,256]{0,1:T(8,128)S(1)} %slice.16), channel_id=1, source_target_pairs={{0,1},{1,2},{2,3},{3,4},{4,5},{5,6},{6,7},{7,8},{8,9},{9,10},{10,1... | collective-permute-start | bytes 1572872 | tf_op jit(solution)/shard_map/ppermute | solution.py:27
  284.3 25.9 %collective-permute-start.1 = (f32[256,768]{0,1:T(8,128)}, f32[256,768]{0,1:T(8,128)}, u32[]{:S(2)}, u32[]{:S(2)}) collective-permute-start(f32[256,768]{0,1:T(8,128)} %bitcast.40), channel_id=1, source_target_pairs={{0,16},{16,32},{32,48},{48,64},{64,80},{80,96},{96,112},{112,128},... | collective-permute-start | bytes 2359304 | tf_op jit(solution)/shard_map/ppermute | solution.py:27
  332.2 215.8 %all-reduce.11.cloned.1.call-start = ((), (), s32[]{:S(2)}) async-start(), calls=%async_computation.7 | async-start | bytes 1572864 | tf_op jit(solution)/shard_map/psum | solution.py:20
  469.2 135.1 %all-reduce.13.cloned.1.call-start = ((), (), s32[]{:S(2)}) async-start(), calls=%async_computation.8 | async-start | bytes 1572864 | tf_op jit(solution)/shard_map/psum | solution.py:20
Sparse Core Ops, SparseCore 0:
  10.4 69.7 all-gather.1
  83.5 82.8 all-reduce.6
  169.3 81.2 all-reduce.8
  332.3 94.3 reduce-scatter.1
  469.3 78.6 all-reduce.10
  550.7 53.5 all-reduce.12
where the time goes:
time: 621 us
  waiting for transfers between devices  494 us (80%)
  blocking collectives  54.5 us (9%)
  matrix products  16.5 us (3%)
  starting transfers between devices  15.4 us (2%)
  local copies, waits for them, and re-layouts  14.8 us (2%)
  between operations  13.6 us (2%)
  other arithmetic  11.7 us (2%)
    psum x4, waiting for transfers between devices, broadcast_by_axis(): value = lax.psum(value, axis)  299 us
    reduce_scatter x1, waiting for transfers between devices, spread(): own = lax.psum_scatter(padded, axis, scatter_dimension=0, tiled=True)  94.5 us
    all_gather x1, waiting for transfers between devices, shards(): rows_local = lax.all_gather(child_panel, 'col', axis=1, tiled=True)[0]  72.9 us
    all_gather x1, blocking collectives, spread(): lax.all_gather(own, axis, axis=0, tiled=True)[:len(lines)]  41.6 us
    ppermute x2, waiting for transfers between devices, shifted(): lax.ppermute(value, axis, [(source, source + steps) for source in range(i...  26.9 us
    ppermute x2, starting transfers between devices, shifted(): lax.ppermute(value, axis, [(source, source + steps) for source in range(i...  15.2 us
  transfers between devices with their start and end apart: 8, of which 8 were waited for; matrix products, arithmetic and copies ran while one was open for 1% of the time, Pallas kernels for 0%

commit v1 on v0

v1 whole, which is shorter than its diff:
```python
import functools

import jax
import jax.numpy as jnp
from jax import lax
from jax.experimental import pallas as pl
from jax.experimental.pallas import tpu as pltpu
from jax.sharding import PartitionSpec as P

BLK = 128
CBD = 4
PBD = 6
HB = 2
PANEL = 512
MESH = pl.DeviceIdType.MESH
F32 = jnp.float32
BF16 = jnp.bfloat16


def halves(value):
    high = value.astype(BF16)
    return high, (value - high.astype(F32)).astype(BF16)


def dot_nt(a, b):
    return lax.dot_general(a, b, (((1,), (1,)), ((), ())), preferred_element_type=F32)


def product_nt(a, b):
    a_high, a_low = a
    b_high, b_low = b
    return dot_nt(a_high, b_high) + (dot_nt(a_high, b_low) + dot_nt(a_low, b_high))


class Links:
    def __init__(self, send_sems, recv_sems):
        self.send_sems, self.recv_sems = send_sems, recv_sems
        self.used = 0
        self.sent = []

    def new(self):
        self.used += 1
        return self.used - 1

    def copy(self, k, src, dst, device):
        return pltpu.make_async_remote_copy(
            src_ref=src,
            dst_ref=dst,
            send_sem=self.send_sems.at[k],
            recv_sem=self.recv_sems.at[k],
            device_id=device,
            device_id_type=MESH,
        )

    def send(self, k, src, dst, device):
        made = self.copy(k, src, dst, device)
        made.start()
        self.sent.append(made)

    def arrived(self, k, ref, device):
        self.copy(k, ref, ref, device).wait_recv()

    def drain(self):
        for made in self.sent:
            made.wait_send()
        self.sent = []


def gather_both(links, place, own, rows_buf, cols_buf, cut):
    s, r, c = place
    z, yl = r // 2, lax.rem(r, 2)
    x, yh = c // 4, lax.rem(c, 4)
    depth = rows_buf.shape[1]
    top, low = pl.ds(0, cut), pl.ds(cut, depth - cut)

    def cy(dx, dy):
        return lax.rem(x + dx + 4, 4) * 4 + lax.rem(yh + dy + 4, 4)

    def rz(dz, flip=0):
        side = 1 - yl if flip else yl
        return lax.rem(z + dz + 8, 8) * 2 + side

    def at_col(j):
        return (s, r, j)

    def at_row(i):
        return (s, i, c)

    yp, ym = at_col(cy(0, 1)), at_col(cy(0, -1))
    xp, xm = at_col(cy(1, 0)), at_col(cy(-1, 0))
    zp, zm = at_row(rz(1)), at_row(rz(-1))
    pair = at_row(rz(0, 1))

    events = []

    def when(t, fn):
        events.append((t, len(events), fn))

    k_yp, k_ym = links.new(), links.new()
    links.send(k_yp, own, rows_buf.at[c], yp)
    links.send(k_ym, own, rows_buf.at[c], ym)
    k_t = links.new()
    transposed = (s, c, r)

    @pl.when(r != c)
    def _():
        links.copy(k_t, own, cols_buf.at[c], transposed).start()

    @pl.when(r == c)
    def _():
        pltpu.make_async_copy(own, cols_buf.at[r], links.recv_sems.at[k_t]).start()

    k_x = {}
    for name in ("own", "-1", "+1", "2"):
        k_x[name] = (links.new(), links.new(), links.new(), links.new())

    def spread_x(name, dy, src=None):
        kp, km, _, _ = k_x[name]
        slot = cy(0, dy)
        src = rows_buf.at[slot] if src is None else src
        links.send(kp, src, rows_buf.at[slot], xp)
        links.send(km, src, rows_buf.at[slot], xm)

    spread_x("own", 0, own)
    k_y2p, k_y2m = links.new(), links.new()

    def from_ym():
        slot = cy(0, -1)
        links.arrived(k_yp, rows_buf.at[slot], ym)
        links.send(k_y2p, rows_buf.at[slot, top], rows_buf.at[slot, top], yp)
        spread_x("-1", -1)

    def from_yp():
        slot = cy(0, 1)
        links.arrived(k_ym, rows_buf.at[slot], yp)
        links.send(k_y2m, rows_buf.at[slot, low], rows_buf.at[slot, low], ym)
        spread_x("+1", 1)

    def far_y():
        slot = cy(0, 2)
        links.arrived(k_y2p, rows_buf.at[slot, top], ym)
        links.arrived(k_y2m, rows_buf.at[slot, low], yp)
        spread_x("2", 2)

    def relay_x(name, dy):
        kp, km, k2p, k2m = k_x[name]
        slot_m, slot_p = cy(-1, dy), cy(1, dy)
        links.arrived(kp, rows_buf.at[slot_m], xm)
        links.send(k2p, rows_buf.at[slot_m, top], rows_buf.at[slot_m, top], xp)
        links.arrived(km, rows_buf.at[slot_p], xp)
        links.send(k2m, rows_buf.at[slot_p, low], rows_buf.at[slot_p, low], xm)

    def far_x(name, dy):
        _, _, k2p, k2m = k_x[name]
        slot = cy(2, dy)
        links.arrived(k2p, rows_buf.at[slot, top], xm)
        links.arrived(k2m, rows_buf.at[slot, low], xp)

    when(5, from_ym)
    when(5, from_yp)
    when(4, lambda: relay_x("own", 0))
    when(10, far_y)
    when(10, lambda: relay_x("-1", -1))
    when(11, lambda: relay_x("+1", 1))
    when(16, lambda: relay_x("2", 2))
    when(90, lambda: [far_x(n, d) for n, d in (("own", 0), ("-1", -1), ("+1", 1), ("2", 2))])

    k_pair = links.new()
    k_z = {(f, d): (links.new(), links.new()) for f in (0, 1) for d in (1, 2, 3, 4)}

    def step_z(flip, d):
        kp, km = k_z[flip, d]
        up, down = cols_buf.at[rz(1 - d, flip)], cols_buf.at[rz(d - 1, flip)]
        if d == 4:
            up, down = up.at[top], down.at[low]
        links.send(kp, up, up, zp)
        links.send(km, down, down, zm)

    def arrive_z(flip, d):
        kp, km = k_z[flip, d]
        from_m, from_p = cols_buf.at[rz(-d, flip)], cols_buf.at[rz(d, flip)]
        if d == 4:
            from_m, from_p = from_m.at[top], from_p.at[low]
        links.arrived(kp, from_m, zm)
        links.arrived(km, from_p, zp)

    def from_transposed():
        links.arrived(k_t, cols_buf.at[r], transposed)
        links.send(k_pair, cols_buf.at[r], cols_buf.at[r], pair)
        step_z(0, 1)

    def from_pair():
        slot = rz(0, 1)
        links.arrived(k_pair, cols_buf.at[slot], pair)
        step_z(1, 1)

    def relay_z(flip, d):
        arrive_z(flip, d)
        if d < 4:
            step_z(flip, d + 1)

    when(7, from_transposed)
    when(9, from_pair)
    for d in (1, 2, 3, 4):
        when(7 + 5 * d, lambda d=d: relay_z(0, d))
        when(9 + 5 * d, lambda d=d: relay_z(1, d))

    for _, _, fn in sorted(events, key=lambda e: e[:2]):
        fn()

    @pl.when(r != c)
    def _():
        links.copy(k_t, own, cols_buf.at[c], transposed).wait_send()


def picks(block_map, child, group):
    weights = {}
    for w in range(CBD + HB):
        i = lax.rem(group * CBD - HB + w + 64, 64)
        mark = block_map[child, i] - group * PBD
        for q in range(max(0, w - HB), min(PBD, w + HB + 1)):
            weights[w, q] = (mark == q).astype(F32)
    return weights


def placed_sum(weights, q, block):
    total = None
    for w in range(CBD + HB):
        if (w, q) in weights:
            term = weights[w, q] * block(w)
            total = term if total is None else total + term
    return total


def kernel(
    front, panel, block_map, parent, inverse, out_ref,
    rows_buf, cols_buf, front_v, parent_v, inverse_v,
    wide, tall, leave, come, assembled, f_out, f_rows, f_cols, out_v,
    a_high, a_low, send_sems, recv_sems, local_sems,
):
    s, r, c = lax.axis_index("sib"), lax.axis_index("row"), lax.axis_index("col")
    place = (s, r, c)
    z, yl = r // 2, lax.rem(r, 2)
    x, yh = c // 4, lax.rem(c, 4)
    links = Links(send_sems, recv_sems)
    sib = (1 - s, r, c)

    loads = [
        pltpu.make_async_copy(src, dst, local_sems.at[k])
        for k, (src, dst) in enumerate(
            ((front.at[0], front_v), (parent, parent_v), (inverse, inverse_v),
             (panel.at[0], rows_buf.at[c]))
        )
    ]
    for load in loads:
        load.start()

    barrier = pltpu.get_barrier_semaphore()

    def greet(device):
        pl.semaphore_signal(barrier, inc=1, device_id=device, device_id_type=MESH)

    def col_at(dx, dy):
        return (s, r, lax.rem(x + dx + 4, 4) * 4 + lax.rem(yh + dy + 4, 4))

    for device in (col_at(0, 1), col_at(0, -1), col_at(1, 0), col_at(-1, 0)):
        greet(device)
    for dz in (1, -1):
        greet((s, lax.rem(z + dz + 8, 8) * 2 + yl, c))
    greet((s, z * 2 + 1 - yl, c))
    greet(sib)
    pl.when(r != c)(lambda: greet((s, c, r)))
    pl.when(c > 0)(lambda: greet((s, r, c - 1)))
    pl.when(r > 0)(lambda: greet((s, r - 1, c)))
    pl.when(c > 0)(lambda: greet((s, r, 0)))
    def one_if(test):
        return test.astype(jnp.int32)

    pl.semaphore_wait(barrier, 8 + one_if(r != c) + one_if(c < 15) + one_if(r < 15) + 15 * one_if(c == 0))

    gather_both(links, place, panel.at[0], rows_buf, cols_buf, 16)
    loads[3].wait()
    loads[0].wait()

    depth = rows_buf.shape[1] * 16
    high, low = halves(rows_buf[...].reshape(depth, rows_buf.shape[2]))
    a_high[...] = high
    a_low[...] = low
    for n in range(2):
        b = halves(cols_buf[8 * n : 8 * n + 8].reshape(depth // 2, cols_buf.shape[2]))
        prod = product_nt((a_high[...], a_low[...]), b)
        for w in range(2):
            col = n * 2 + w
            wide[HB + col] = front_v[:, col * BLK : (col + 1) * BLK] - prod[:, w * BLK : (w + 1) * BLK]

    k_col = links.new()
    tail, head = wide.at[pl.ds(CBD, HB)], wide.at[pl.ds(0, HB)]
    col_copy = links.copy(k_col, tail, head, (s, r, lax.rem(c + 1, 16)))
    pl.when(c < 15)(col_copy.start)
    pl.when(c > 0)(col_copy.wait_recv)

    edge = HB * BLK

    @pl.when(c == 0)
    def _():
        wide[0:HB] = jnp.zeros((HB,) + wide.shape[1:], F32)

    @pl.when(r == 0)
    def _():
        tall[:, 0:edge, :] = jnp.zeros((PBD, edge, BLK), F32)

    pick = picks(block_map, s, c)
    for q in range(PBD):
        tall[q, edge:, :] = placed_sum(pick, q, lambda w: wide[w])

    k_row = links.new()
    width = pl.ds(0, PBD)
    row_copy = links.copy(
        k_row, tall.at[width, pl.ds(CBD * BLK, edge)], tall.at[width, pl.ds(0, edge)],
        (s, lax.rem(r + 1, 16), c),
    )
    pl.when(r < 15)(row_copy.start)
    pl.when(r > 0)(row_copy.wait_recv)

    pick = picks(block_map, s, r)
    half = PBD // 2
    k_sib = links.new()

    def blocks(q):
        return lambda w: tall[q, w * BLK : (w + 1) * BLK, :]

    for k in range(PBD):
        for q in range(PBD):
            leave[k, q] = placed_sum(pick, k, blocks(q))
    links.send(k_sib, leave.at[pl.ds(half * (1 - s), half)], come, sib)
    loads[1].wait()
    for k in range(half):
        for q in range(PBD):
            at = (slice(k * BLK, (k + 1) * BLK), slice(q * BLK, (q + 1) * BLK))
            assembled[at] = parent_v[at] + leave[half * s + k, q]
    links.arrived(k_sib, come, sib)
    for k in range(half):
        for q in range(PBD):
            at = (slice(k * BLK, (k + 1) * BLK), slice(q * BLK, (q + 1) * BLK))
            assembled[at] += come[k, q]

    loads[2].wait()
    k_scatter = [links.new() for _ in range(16)]

    @pl.when(c == 0)
    def _():
        factor = product_nt(halves(assembled[:, :PANEL]), halves(inverse_v[...]))
        f_out[...] = factor.reshape(f_rows.shape)
        f_rows[0] = f_out[0]
        copies = [
            pltpu.make_async_remote_copy(
                src_ref=f_out.at[j], dst_ref=f_rows.at[j],
                send_sem=links.send_sems.at[k_scatter[j]], recv_sem=links.recv_sems.at[k_scatter[0]],
                device_id=(s, r, jnp.int32(j)), device_id_type=MESH)
            for j in range(1, 16)
        ]
        for made in copies:
            made.start()
        for made in copies:
            made.wait_send()

    @pl.when(c > 0)
    def _():
        links.arrived(k_scatter[0], f_rows.at[c], (s, r, 0))

    gather_both(links, place, f_rows.at[c], f_rows, f_cols.at[s], 8)
    k_swap = links.new()
    links.send(k_swap, f_cols.at[s], f_cols.at[s], sib)
    links.arrived(k_swap, f_cols.at[1 - s], sib)

    f_all = f_rows[...].reshape(assembled.shape[0], PANEL)
    g_all = f_cols[...].reshape(assembled.shape[1], PANEL)
    fh = halves(f_all)
    parent_rows, parent_cols = assembled.shape
    for n in range(3):
        span = slice(n * 256, (n + 1) * 256)
        prod = product_nt(fh, halves(g_all[span]))
        row_at = (r * 2 + s) * parent_rows + lax.broadcasted_iota(jnp.int32, prod.shape, 0)
        col_at_ = c * parent_cols + n * 256 + lax.broadcasted_iota(jnp.int32, prod.shape, 1)
        inside = (row_at >= PANEL) & (col_at_ >= PANEL)
        now = assembled[:, span]
        done = jnp.where(inside, now - prod, now)
        if n < 2:
            done = jnp.where(c == 0, f_all[:, span], done)
        out_v[:, span] = done
    store = pltpu.make_async_copy(out_v, out_ref, local_sems.at[0])
    store.start()

    links.drain()
    pl.when(c < 15)(col_copy.wait_send)
    pl.when(r < 15)(row_copy.wait_send)
    store.wait()
    assert links.used <= 144, links.used


def shards(front, panel, block_map, parent, inverse):
    anywhere = pl.BlockSpec(memory_space=pl.ANY)
    rows, cols = parent.shape
    kc = panel.shape[2]
    return pl.pallas_call(
        kernel,
        out_shape=jax.ShapeDtypeStruct(parent.shape, F32),
        in_specs=[anywhere, anywhere, pl.BlockSpec(memory_space=pltpu.SMEM), anywhere, anywhere],
        out_specs=anywhere,
        scratch_shapes=[
            pltpu.VMEM((16, 32, kc), F32),
            pltpu.VMEM((16, 32, kc), F32),
            pltpu.VMEM((512, 512), F32),
            pltpu.VMEM((rows, cols), F32),
            pltpu.VMEM((PANEL, PANEL), F32),
            pltpu.VMEM((CBD + HB, 512, BLK), F32),
            pltpu.VMEM((PBD, 768, BLK), F32),
            pltpu.VMEM((PBD, PBD, BLK, BLK), F32),
            pltpu.VMEM((3, PBD, BLK, BLK), F32),
            pltpu.VMEM((rows, cols), F32),
            pltpu.VMEM((16, 24, PANEL), F32),
            pltpu.VMEM((16, 24, PANEL), F32),
            pltpu.VMEM((2, 16, 24, PANEL), F32),
            pltpu.VMEM((rows, cols), F32),
            pltpu.VMEM((512, kc), BF16),
            pltpu.VMEM((512, kc), BF16),
            pltpu.SemaphoreType.DMA((144,)),
            pltpu.SemaphoreType.DMA((144,)),
            pltpu.SemaphoreType.DMA((4,)),
        ],
        compiler_params=pltpu.CompilerParams(
            collective_id=0, has_side_effects=True, vmem_limit_bytes=50 * 2**20
        ),
        name="front_step",
    )(front, panel, block_map, parent, inverse)


def solution(mesh):
    placed = (
        P("sib", "row", "col"), P("sib", ("row", "col"), None), P(),
        P(("row", "sib"), "col"), P(),
    )
    return jax.shard_map(
        shards, mesh=mesh, in_specs=placed, out_specs=P(("row", "sib"), "col"), check_vma=False
    )
```

time: 621 us -> 147 us (0.24)
  waiting for transfers between devices: 494 us -> 0 us
  Pallas kernels: 0 us -> 139 us
  blocking collectives: 54.5 us -> 0 us
  matrix products: 16.5 us -> 0 us
  starting transfers between devices: 15.4 us -> 0 us
  between operations: 13.6 us -> 0.01 us
  other arithmetic: 11.7 us -> 0 us
  local copies, waits for them, and re-layouts: 14.8 us -> 5.05 us
    psum x4 -> x0, waiting for transfers between devices: 299 us -> none  [broadcast_by_axis(): value = lax.psum(value, axis)]
    pallas_call x0 -> x1, Pallas kernels: none -> 139 us  [shards(): pl.pallas_call(kernel, out_shape=jax.ShapeDtypeStruct(parent.shape, F32),...]
    reduce_scatter x1 -> x0, waiting for transfers between devices: 94.5 us -> none  [spread(): own = lax.psum_scatter(padded, axis, scatter_dimension=0, tiled=True)]
    all_gather x1 -> x0, waiting for transfers between devices: 72.9 us -> none  [shards(): rows_local = lax.all_gather(child_panel, 'col', axis=1, tiled=True)[0]]
    all_gather x1 -> x0, blocking collectives: 41.6 us -> none  [spread(): lax.all_gather(own, axis, axis=0, tiled=True)[:len(lines)]]
    ppermute x2 -> x0, waiting for transfers between devices: 26.9 us -> none  [shifted(): lax.ppermute(value, axis, [(source, source + steps) for source in range(i...]
    dot_general x5 -> x0, matrix products: 16.5 us -> none  [the longest x1 5.42 us: shards(): lax.dot_general(rows_local, cols_local, (((1,), (1,)), ((), ())), precisi...]
    ppermute x2 -> x0, starting transfers between devices: 15.2 us -> none  [shifted(): lax.ppermute(value, axis, [(source, source + steps) for source in range(i...]
  transfers between devices with their start and end apart: 8 -> 0, of which waited for: 8 -> 0; matrix products, arithmetic and copies ran while one was open for 1% -> 0% of each run, Pallas kernels for 0% -> 0%
where the time goes in v1:
time: 147 us; the launch traced here: 144 us
  Pallas kernels  139 us (95%)
  local copies, waits for them, and re-layouts  5.05 us (3%)
    pallas_call x1, Pallas kernels, shards(): pl.pallas_call(kernel, out_shape=jax.ShapeDtypeStruct(parent.shape, F32),...  139 us
    unnamed x9, local copies, waits for them, and re-layouts  5.05 us

profile of v1, /device:TPU:1, one launch (start us, length us, event | category | flops | bytes accessed | tf_op | source)
XLA Modules:
  0.0 144.2 jit_solution(14789693860460633372)
XLA Ops:
  0.0 0.0 copy-start
  0.0 1.2 copy-done
  1.2 0.0 copy-start.1
  1.2 1.2 copy-done.1
  2.5 0.0 copy-start.2
  2.5 0.9 copy-done.2
  3.4 0.0 copy-start.3
  3.4 0.7 copy-done.3
  4.0 139.1 %front_step.1 = f32[384,768]{1,0:T(8,128)S(1)} custom-call(f32[1,512,512]{2,1,0:T(8,128)S(1)} %copy-done, f32[1,32,1024]{2,1,0:T(8,128)S(1)} %copy-done.2, s32[2,64]{1,0:T(2,128)S(1)} %copy-done.3, f32[384,768]{1,0:T(8,128)} %parent.1, f32[512,512]{1,0:T(8,128)S(1)} %copy-done.1), custom_call_target="tpu_custom_call" | custom-call | tf_op jit(solution)/shard_map/front_step/pallas_call | solution.py:405
  143.2 1.0 copy.7
Async XLA Ops:
  0.0 1.2 copy-start
  1.2 1.2 copy-start.1
  2.5 0.9 copy-start.2
  3.4 0.7 copy-start.3

commit v2 on v1

v2 whole, which is shorter than its diff:
```python
import functools

import jax
import jax.numpy as jnp
from jax import lax
from jax.experimental import pallas as pl
from jax.experimental.pallas import tpu as pltpu
from jax.sharding import PartitionSpec as P

BLK = 128
CBD = 4
PBD = 6
HB = 2
PANEL = 512
MESH = pl.DeviceIdType.MESH
F32 = jnp.float32
BF16 = jnp.bfloat16


def halves(value):
    high = value.astype(BF16)
    return high, (value - high.astype(F32)).astype(BF16)


def dot_nt(a, b):
    return lax.dot_general(a, b, (((1,), (1,)), ((), ())), preferred_element_type=F32)


def product_nt(a, b):
    a_high, a_low = a
    b_high, b_low = b
    return dot_nt(a_high, b_high) + (dot_nt(a_high, b_low) + dot_nt(a_low, b_high))


class Links:
    def __init__(self, send_sems, recv_sems):
        self.send_sems, self.recv_sems = send_sems, recv_sems
        self.used = 0
        self.sent = []

    def new(self):
        self.used += 1
        return self.used - 1

    def copy(self, k, src, dst, device, k_recv=None):
        return pltpu.make_async_remote_copy(
            src_ref=src,
            dst_ref=dst,
            send_sem=self.send_sems.at[k],
            recv_sem=self.recv_sems.at[k if k_recv is None else k_recv],
            device_id=device,
            device_id_type=MESH,
        )

    def send(self, k, src, dst, device):
        made = self.copy(k, src, dst, device)
        made.start()
        self.sent.append(made)

    def arrived(self, k, ref, device):
        self.copy(k, ref, ref, device).wait_recv()

    def drain(self):
        for made in self.sent:
            made.wait_send()
        self.sent = []


class Ring:
    def __init__(self, links, place):
        self.links = links
        self.s, self.r, self.c = s, r, c = place
        self.z, self.yl = r // 2, lax.rem(r, 2)
        self.x, self.yh = c // 4, lax.rem(c, 4)
        self.yp, self.ym = self.at_col(self.cy(0, 1)), self.at_col(self.cy(0, -1))
        self.xp, self.xm = self.at_col(self.cy(1, 0)), self.at_col(self.cy(-1, 0))
        self.zp, self.zm = self.at_row(self.rz(1)), self.at_row(self.rz(-1))
        self.pair = self.at_row(self.rz(0, 1))
        self.sib = (1 - s, r, c)
        self.events = []

    def cy(self, dx, dy):
        return lax.rem(self.x + dx + 4, 4) * 4 + lax.rem(self.yh + dy + 4, 4)

    def rz(self, dz, flip=0):
        side = 1 - self.yl if flip else self.yl
        return lax.rem(self.z + dz + 8, 8) * 2 + side

    def at_col(self, j):
        return (self.s, self.r, j)

    def at_row(self, i):
        return (self.s, i, self.c)

    def when(self, t, fn):
        self.events.append((t, len(self.events), fn))

    def run(self, until=1e9):
        ready = sorted((e for e in self.events if e[0] < until), key=lambda e: e[:2])
        self.events = [e for e in self.events if e[0] >= until]
        for _, _, fn in ready:
            fn()


def gather_rows(ring, own, rows_buf, cut, times):
    links, c = ring.links, ring.c
    cy, yp, ym, xp, xm = ring.cy, ring.yp, ring.ym, ring.xp, ring.xm
    depth = rows_buf.shape[1]
    top, low = pl.ds(0, cut), pl.ds(cut, depth - cut)
    k_yp, k_ym = links.new(), links.new()
    links.send(k_yp, own, rows_buf.at[c], yp)
    links.send(k_ym, own, rows_buf.at[c], ym)
    k_x = {}
    for dy in (0, -1, 1, 2):
        k_x[dy] = (links.new(), links.new(), links.new(), links.new())

    def spread_x(dy, src=None):
        kp, km, _, _ = k_x[dy]
        slot = cy(0, dy)
        src = rows_buf.at[slot] if src is None else src
        links.send(kp, src, rows_buf.at[slot], xp)
        links.send(km, src, rows_buf.at[slot], xm)

    spread_x(0, own)
    k_y2p, k_y2m = links.new(), links.new()

    def from_ym():
        slot = cy(0, -1)
        links.arrived(k_yp, rows_buf.at[slot], ym)
        links.send(k_y2p, rows_buf.at[slot, top], rows_buf.at[slot, top], yp)
        spread_x(-1)

    def from_yp():
        slot = cy(0, 1)
        links.arrived(k_ym, rows_buf.at[slot], yp)
        links.send(k_y2m, rows_buf.at[slot, low], rows_buf.at[slot, low], ym)
        spread_x(1)

    def far_y():
        slot = cy(0, 2)
        links.arrived(k_y2p, rows_buf.at[slot, top], ym)
        links.arrived(k_y2m, rows_buf.at[slot, low], yp)
        spread_x(2)

    def relay_x(dy):
        kp, km, k2p, k2m = k_x[dy]
        slot_m, slot_p = cy(-1, dy), cy(1, dy)
        links.arrived(kp, rows_buf.at[slot_m], xm)
        links.send(k2p, rows_buf.at[slot_m, top], rows_buf.at[slot_m, top], xp)
        links.arrived(km, rows_buf.at[slot_p], xp)
        links.send(k2m, rows_buf.at[slot_p, low], rows_buf.at[slot_p, low], xm)

    def far_x(dy):
        _, _, k2p, k2m = k_x[dy]
        slot = cy(2, dy)
        links.arrived(k2p, rows_buf.at[slot, top], xm)
        links.arrived(k2m, rows_buf.at[slot, low], xp)

    ring.when(times[0], from_ym)
    ring.when(times[0], from_yp)
    ring.when(times[1], lambda: relay_x(0))
    ring.when(times[2], far_y)
    ring.when(times[3], lambda: relay_x(-1))
    ring.when(times[4], lambda: relay_x(1))
    ring.when(times[5], lambda: relay_x(2))
    ring.when(times[6], lambda: [far_x(dy) for dy in (0, -1, 1, 2)])


def gather_cols_ring(ring, first, cols_buf, t, gap, end):
    links = ring.links
    rz, pair, zp, zm = ring.rz, ring.pair, ring.zp, ring.zm
    depth = cols_buf.shape[1]
    cut = depth // 16 * 8
    parts = (pl.ds(0, cut), pl.ds(cut, depth - cut))
    k_pair = links.new()
    k_z = {(flip, d): (links.new(), links.new()) for flip in (0, 1) for d in (1, 2, 3, 4)}

    def piece(dz, flip, d, way):
        ref = cols_buf.at[rz(dz, flip)]
        return ref.at[parts[way < 0]] if d == 4 else ref

    def step(flip, d):
        for way, k in zip((1, -1), k_z[flip, d]):
            ref = piece(way * (1 - d), flip, d, way)
            links.send(k, ref, ref, zp if way > 0 else zm)

    def relay(flip, d):
        for way, k in zip((1, -1), k_z[flip, d]):
            links.arrived(k, piece(-way * d, flip, d, way), zm if way > 0 else zp)
            if d < 4:
                ref = piece(-way * d, flip, d + 1, way)
                links.send(k_z[flip, d + 1][way < 0], ref, ref, zp if way > 0 else zm)

    def from_first():
        first()
        ref = cols_buf.at[rz(0)]
        links.send(k_pair, ref, ref, pair)
        step(0, 1)

    def from_pair():
        links.arrived(k_pair, cols_buf.at[rz(0, 1)], pair)
        step(1, 1)

    ring.when(t, from_first)
    ring.when(t + gap / 2, from_pair)
    for d in (1, 2, 3, 4):
        ring.when(end if d == 4 else t + gap * d, lambda d=d: relay(0, d))
        ring.when(end if d == 4 else t + gap * (d + 0.5), lambda d=d: relay(1, d))


def gather_cols_two(ring, first, cols_buf, come_buf, times):
    links, yl = ring.links, ring.yl
    rz, pair, sib = ring.rz, ring.pair, ring.sib
    depth = cols_buf.shape[1]
    cut = depth // 16 * 8
    parts = {1: pl.ds(0, cut), -1: pl.ds(cut, depth - cut)}
    k_pair = links.new()
    k_z = {(flip, d): links.new() for flip in (0, 1) for d in (1, -1, 2, -2, 3, -3, 4, -4)}
    k_sib = {(flip, d): links.new() for flip in (0, 1) for d in range(-3, 5)}

    def piece(flip, d):
        ref = cols_buf.at[rz(-d, flip)]
        return ref.at[parts[1 if d > 0 else -1]] if abs(d) == 4 else ref

    def arrived(flip, d):
        links.arrived(k_z[flip, d], piece(flip, d), ring.at_row(rz(-d, flip if abs(d) < 3 else 0)))

    def to_sib(flip, d):
        links.send(k_sib[flip, d], cols_buf.at[rz(d, flip)], cols_buf.at[rz(d, flip)], sib)

    def from_first():
        first()
        ref = cols_buf.at[rz(0)]
        for d in (2, -2, 1, -1):
            for flip in (1, 0):
                links.send(k_z[flip, d], ref, ref, ring.at_row(rz(d, flip)))
        links.send(k_pair, ref, ref, pair)
        to_sib(0, 0)

    def from_near(d):
        for flip in (0, 1):
            arrived(flip, d)
            if abs(d) == 2:
                for e in (3, 4):
                    way = 1 if d > 0 else -1
                    ref = cols_buf.at[rz(-d, flip)]
                    ref = ref.at[parts[way]] if e == 4 else ref
                    links.send(k_z[flip, way * e], ref, ref, ring.at_row(rz(way * (e - 2))))
            to_sib(flip, -d)

    def from_pair():
        links.arrived(k_pair, cols_buf.at[rz(0, 1)], pair)
        to_sib(1, 0)

    def from_far():
        for flip in (0, 1):
            for d in (3, -3):
                arrived(flip, d)
                to_sib(flip, -d)
        for flip in (0, 1):
            arrived(flip, 4)
            arrived(flip, -4)
            to_sib(flip, 4)

    def from_sib():
        for (flip, d), k in k_sib.items():
            links.arrived(k, come_buf.at[rz(d, flip)], sib)

    ring.when(times[0], from_first)
    for d in (2, -2):
        ring.when(times[1], lambda d=d: from_near(d))
    ring.when(times[2], from_pair)
    for d in (1, -1):
        ring.when(times[2], lambda d=d: from_near(d))
    ring.when(times[3], from_far)
    ring.when(times[4], from_sib)


def transpose_whole(ring, own, cols_buf):
    links, s, r, c = ring.links, ring.s, ring.r, ring.c
    k = links.new()
    there = (s, c, r)

    @pl.when(r != c)
    def _():
        links.copy(k, own, cols_buf.at[c], there).start()

    @pl.when(r == c)
    def _():
        pltpu.make_async_copy(own, cols_buf.at[r], links.recv_sems.at[k]).start()

    def sent():
        @pl.when(r != c)
        def _():
            links.copy(k, own, cols_buf.at[c], there).wait_send()

    return (lambda: links.arrived(k, cols_buf.at[r], there)), sent


def transpose_parts(ring, own, cols_buf):
    links, s, r, c = ring.links, ring.s, ring.r, ring.c
    k = [links.new(), links.new()]
    k_send = [links.new(), links.new()]
    part, at = c // 8, lax.rem(c, 8)
    rows = [pl.ds(0, 16), pl.ds(16, 16)]

    def here(h):
        return (r == c) & (at * 2 + h == r)

    def copy(h, p):
        return links.copy(k_send[h], own.at[rows[h]], cols_buf.at[p, at * 2 + h], (s, at * 2 + h, r), k[p])

    for h in (0, 1):
        for p in (0, 1):

            @pl.when(jnp.logical_not(here(h)) & (part == p))
            def _():
                copy(h, p).start()

            @pl.when(here(h) & (part == p))
            def _():
                pltpu.make_async_copy(own.at[rows[h]], cols_buf.at[p, r], links.recv_sems.at[k[p]]).start()

    def sent():
        for h in (0, 1):

            @pl.when(jnp.logical_not(here(h)))
            def _():
                copy(h, 0).wait_send()

    def arrived(p):
        return lambda: links.arrived(k[p], cols_buf.at[p, r], (s, c, p * 8 + ring.z))

    return arrived, sent


def picks(block_map, child, group):
    weights = {}
    for w in range(CBD + HB):
        i = lax.rem(group * CBD - HB + w + 64, 64)
        mark = block_map[child, i] - group * PBD
        for q in range(max(0, w - HB), min(PBD, w + HB + 1)):
            weights[w, q] = (mark == q).astype(F32)
    return weights


def placed_sum(weights, q, block):
    total = None
    for w in range(CBD + HB):
        if (w, q) in weights:
            term = weights[w, q] * block(w)
            total = term if total is None else total + term
    return total


def kernel(
    front, panel, block_map, parent, inverse, out_ref,
    rows_buf, cols_buf, front_v, parent_v, inverse_v,
    wide, tall, leave, come, assembled, f_out, f_rows, f_cols, out_v,
    a_high, a_low, send_sems, recv_sems, local_sems,
):
    s, r, c = lax.axis_index("sib"), lax.axis_index("row"), lax.axis_index("col")
    place = (s, r, c)
    z, yl = r // 2, lax.rem(r, 2)
    x, yh = c // 4, lax.rem(c, 4)
    links = Links(send_sems, recv_sems)
    sib = (1 - s, r, c)

    loads = [
        pltpu.make_async_copy(src, dst, local_sems.at[k])
        for k, (src, dst) in enumerate(
            ((front.at[0], front_v), (parent, parent_v), (inverse, inverse_v),
             (panel.at[0], rows_buf.at[c]))
        )
    ]
    for load in loads:
        load.start()

    barrier = pltpu.get_barrier_semaphore()

    def greet(device):
        pl.semaphore_signal(barrier, inc=1, device_id=device, device_id_type=MESH)

    ring = Ring(links, place)
    for device in (ring.yp, ring.ym, ring.xp, ring.xm, ring.pair, sib):
        greet(device)
    for dz in (1, -1, 2, -2):
        for flip in (0, 1):
            greet(ring.at_row(ring.rz(dz, flip)))
    end_low, end_high = (r == 0) & (c == 0), (r == 15) & (c == 15)
    pl.when(jnp.logical_not(end_low))(lambda: greet((s, c, z)))
    pl.when(jnp.logical_not(end_high))(lambda: greet((s, c, 8 + z)))
    pl.when(r != c)(lambda: greet((s, c, r)))
    pl.when(c > 0)(lambda: greet((s, r, c - 1)))
    pl.when(r > 0)(lambda: greet((s, r - 1, c)))
    pl.when(c > 0)(lambda: greet((s, r, 0)))

    def one_if(test):
        return test.astype(jnp.int32)

    pl.semaphore_wait(
        barrier,
        16 - one_if(end_low) - one_if(end_high) + one_if(r != c) + one_if(c < 15)
        + one_if(r < 15) + 15 * one_if(c == 0),
    )

    cols_from, cols_sent = transpose_parts(ring, panel.at[0], cols_buf)
    gather_rows(ring, panel.at[0], rows_buf, 16, (5, 4.5, 10, 11, 12, 17, 99))
    gather_cols_ring(ring, cols_from(1), cols_buf.at[1], 8, 5, 100)
    gather_cols_ring(ring, cols_from(0), cols_buf.at[0], 13.2, 5, 190)
    ring.run(until=150)
    loads[3].wait()
    loads[0].wait()
    high, low = halves(rows_buf[...].reshape(512, rows_buf.shape[2]))
    a_high[...] = high
    a_low[...] = low

    def update(part):
        b = halves(cols_buf[part].reshape(256, cols_buf.shape[3]))
        prod = product_nt((a_high[...], a_low[...]), b)
        for w in range(2):
            col = part * 2 + w
            wide[HB + col] = front_v[:, col * BLK : (col + 1) * BLK] - prod[:, w * BLK : (w + 1) * BLK]

    edge = HB * BLK
    half = PBD // 2
    col_pick, row_pick = picks(block_map, s, c), picks(block_map, s, r)
    k_col, k_scatter = links.new(), links.new()
    k_row = [links.new() for _ in range(PBD)]
    k_sib = [links.new(), links.new()]
    spans = ((0, 4), (4, PBD))
    k_scatter_send = [links.new() for _ in range(15)]
    col_to, col_from = (s, r, lax.rem(c + 1, 16)), (s, r, lax.rem(c + 15, 16))
    row_to, row_from = (s, lax.rem(r + 1, 16), c), (s, lax.rem(r + 15, 16), c)

    def col_copy(device):
        return links.copy(k_col, wide.at[pl.ds(CBD, HB)], wide.at[pl.ds(0, HB)], device)

    def row_copies(device, span):
        return [
            links.copy(
                k_row[q], tall.at[q, pl.ds(CBD * BLK, edge)], tall.at[q, pl.ds(0, edge)], device
            )
            for q in range(*span)
        ]

    def spread_cols():
        for q in range(PBD):
            tall[q, edge:, :] = placed_sum(col_pick, q, lambda w: wide[w])

    def send_rows(span):
        @pl.when(r < 15)
        def _():
            for made in row_copies(row_to, span):
                made.start()

    def sib_copy(part):
        first, last = spans[part]
        cols = pl.ds(first, last - first)
        return links.copy(
            k_sib[part], leave.at[pl.ds(half * (1 - s), half), cols],
            come.at[pl.ds(0, half), cols], sib,
        )

    def spread_rows(part):
        @pl.when(r > 0)
        def _():
            for made in row_copies(row_from, spans[part]):
                made.wait_recv()

        for k in range(PBD):
            for q in range(*spans[part]):
                leave[k, q] = placed_sum(
                    row_pick, k, lambda w: tall[q, w * BLK : (w + 1) * BLK, :]
                )
        sib_copy(part).start()

    def assemble(part):
        sib_copy(part).wait_recv()
        for k in range(half):
            for q in range(*spans[part]):
                at = (slice(k * BLK, (k + 1) * BLK), slice(q * BLK, (q + 1) * BLK))
                assembled[at] = parent_v[at] + (leave[half * s + k, q] + come[k, q])

    update(1)
    pl.when((c < 15) & ((c > 0) | (yl == 1)))(lambda: col_copy(col_to).start())
    ring.run()
    update(0)

    @pl.when(r == 0)
    def _():
        tall[:, 0:edge, :] = jnp.zeros((PBD, edge, BLK), F32)

    def scatter(j):
        return links.copy(
            k_scatter_send[j - 1], f_out.at[j], f_rows.at[j], (s, r, jnp.int32(j)), k_scatter
        )

    loads[1].wait()
    loads[2].wait()

    @pl.when(c == 0)
    def _():
        wide[0:HB] = jnp.zeros((HB,) + wide.shape[1:], F32)
        spread_cols()
        send_rows(spans[0])
        pl.when(yl == 0)(lambda: col_copy(col_to).start())
        spread_rows(0)
        assemble(0)
        factor = product_nt(halves(assembled[:, :PANEL]), halves(inverse_v[...]))
        f_out[...] = factor.reshape(f_rows.shape)
        f_rows[0] = f_out[0]
        for j in range(1, 16):
            scatter(j).start()

    def from_col():
        col_copy(col_from).wait_recv()
        spread_cols()
        send_rows(spans[0])

    pl.when(c > 1)(from_col)

    @pl.when(c > 0)
    def _():
        links.copy(k_scatter, f_rows.at[c], f_rows.at[c], (s, r, 0)).wait_recv()

    own = f_rows.at[c]
    cols_here, own_sent = transpose_whole(ring, own, f_cols.at[s])
    gather_rows(ring, own, f_rows, 8, (4, 3.5, 7.5, 7.6, 7.7, 11, 80))
    gather_cols_two(ring, cols_here, f_cols.at[s], f_cols.at[1 - s], (6, 10, 12, 60, 190))
    ring.when(0.1, lambda: pl.when(c == 1)(from_col))
    ring.when(12.5, lambda: send_rows(spans[1]))

    ring.when(50, lambda: pl.when(c > 0)(lambda: spread_rows(0)))
    ring.when(70, lambda: spread_rows(1))
    ring.when(100, lambda: pl.when(c > 0)(lambda: assemble(0)))
    ring.when(100, lambda: assemble(1))
    ring.run()

    f_all = f_rows[...].reshape(assembled.shape[0], PANEL)
    g_all = f_cols[...].reshape(assembled.shape[1], PANEL)
    fh = halves(f_all)
    parent_rows, parent_cols = assembled.shape
    for n in range(3):
        span = slice(n * 256, (n + 1) * 256)
        prod = product_nt(fh, halves(g_all[span]))
        row_at = (r * 2 + s) * parent_rows + lax.broadcasted_iota(jnp.int32, prod.shape, 0)
        col_at_ = c * parent_cols + n * 256 + lax.broadcasted_iota(jnp.int32, prod.shape, 1)
        inside = (row_at >= PANEL) & (col_at_ >= PANEL)
        now = assembled[:, span]
        done = jnp.where(inside, now - prod, now)
        if n < 2:
            done = jnp.where(c == 0, f_all[:, span], done)
        out_v[:, span] = done
    store = pltpu.make_async_copy(out_v, out_ref, local_sems.at[0])
    store.start()

    links.drain()
    cols_sent()
    own_sent()
    pl.when(c < 15)(lambda: col_copy(col_to).wait_send())

    @pl.when(r < 15)
    def _():
        for made in row_copies(row_to, (0, PBD)):
            made.wait_send()

    for part in (0, 1):
        sib_copy(part).wait_send()

    @pl.when(c == 0)
    def _():
        for j in range(1, 16):
            scatter(j).wait_send()

    store.wait()
    assert links.used <= 160, links.used


def shards(front, panel, block_map, parent, inverse):
    anywhere = pl.BlockSpec(memory_space=pl.ANY)
    rows, cols = parent.shape
    kc = panel.shape[2]
    return pl.pallas_call(
        kernel,
        out_shape=jax.ShapeDtypeStruct(parent.shape, F32),
        in_specs=[anywhere, anywhere, pl.BlockSpec(memory_space=pltpu.SMEM), anywhere, anywhere],
        out_specs=anywhere,
        scratch_shapes=[
            pltpu.VMEM((16, 32, kc), F32),
            pltpu.VMEM((2, 16, 16, kc), F32),
            pltpu.VMEM((512, 512), F32),
            pltpu.VMEM((rows, cols), F32),
            pltpu.VMEM((PANEL, PANEL), F32),
            pltpu.VMEM((CBD + HB, 512, BLK), F32),
            pltpu.VMEM((PBD, 768, BLK), F32),
            pltpu.VMEM((PBD, PBD, BLK, BLK), F32),
            pltpu.VMEM((3, PBD, BLK, BLK), F32),
            pltpu.VMEM((rows, cols), F32),
            pltpu.VMEM((16, 24, PANEL), F32),
            pltpu.VMEM((16, 24, PANEL), F32),
            pltpu.VMEM((2, 16, 24, PANEL), F32),
            pltpu.VMEM((rows, cols), F32),
            pltpu.VMEM((512, kc), BF16),
            pltpu.VMEM((512, kc), BF16),
            pltpu.SemaphoreType.DMA((160,)),
            pltpu.SemaphoreType.DMA((160,)),
            pltpu.SemaphoreType.DMA((4,)),
        ],
        compiler_params=pltpu.CompilerParams(
            collective_id=0, has_side_effects=True, vmem_limit_bytes=60 * 2**20
        ),
        name="front_step",
    )(front, panel, block_map, parent, inverse)


def solution(mesh):
    placed = (
        P("sib", "row", "col"), P("sib", ("row", "col"), None), P(),
        P(("row", "sib"), "col"), P(),
    )
    return jax.shard_map(
        shards, mesh=mesh, in_specs=placed, out_specs=P(("row", "sib"), "col"), check_vma=False
    )
```

time: 147 us -> 139 us (0.946)
  the two profiles are of different devices: /device:TPU:1 before, /device:TPU:17 now
where the time goes in v2:
time: 139 us; the launch traced here: 138 us
  Pallas kernels  136 us (98%)
  local copies, waits for them, and re-layouts  2.36 us (2%)
    pallas_call x1, Pallas kernels, shards(): pl.pallas_call(kernel, out_shape=jax.ShapeDtypeStruct(parent.shape, F32),...  136 us

profile of v2, /device:TPU:17, one launch (start us, length us, event | category | flops | bytes accessed | tf_op | source)
XLA Modules:
  0.0 138.4 jit_solution(2139866433390250244)
XLA Ops:
  0.0 136.1 %front_step.1 = f32[384,768]{1,0:T(8,128)} custom-call(f32[1,512,512]{2,1,0:T(8,128)} %front.1, f32[1,32,1024]{2,1,0:T(8,128)} %panel.1, s32[2,64]{1,0:T(2,128)} %block_map.1, f32[384,768]{1,0:T(8,128)} %parent.1, f32[512,512]{1,0:T(8,128)} %inverse.1), custom_call_target="tpu_custom_call" | custom-call | tf_op jit(solution)/shard_map/front_step/pallas_call | solution.py:584
  136.1 2.4 %copy.7 = f32[384,768]{1,0:T(8,128)} copy(f32[384,768]{1,0:T(8,128)} %front_step.1) | data formatting | bytes 2359296

commit v3 on v2

--- a/solution.py
+++ b/solution.py
@@ -356,7 +356,7 @@
 def kernel(
     front, panel, block_map, parent, inverse, out_ref,
     rows_buf, cols_buf, front_v, parent_v, inverse_v,
-    wide, tall, leave, come, assembled, f_out, f_rows, f_cols, out_v,
+    wide, tall, edge_in, leave, come, assembled, f_out, f_rows, f_cols, out_v,
     a_high, a_low, send_sems, recv_sems, local_sems,
 ):
     s, r, c = lax.axis_index("sib"), lax.axis_index("row"), lax.axis_index("col")
@@ -405,9 +405,10 @@
     )
 
     cols_from, cols_sent = transpose_parts(ring, panel.at[0], cols_buf)
-    gather_rows(ring, panel.at[0], rows_buf, 16, (5, 4.5, 10, 11, 12, 17, 99))
     gather_cols_ring(ring, cols_from(1), cols_buf.at[1], 8, 5, 100)
     gather_cols_ring(ring, cols_from(0), cols_buf.at[0], 13.2, 5, 190)
+    ring.run(until=13.3)
+    gather_rows(ring, panel.at[0], rows_buf, 16, (19, 18.5, 24, 25, 26, 31, 99))
     ring.run(until=150)
     loads[3].wait()
     loads[0].wait()
@@ -427,6 +428,7 @@
     col_pick, row_pick = picks(block_map, s, c), picks(block_map, s, r)
     k_col, k_scatter = links.new(), links.new()
     k_row = [links.new() for _ in range(PBD)]
+    k_edge = [links.new(), links.new()]
     k_sib = [links.new(), links.new()]
     spans = ((0, 4), (4, PBD))
     k_scatter_send = [links.new() for _ in range(15)]
@@ -448,8 +450,26 @@
         for q in range(PBD):
             tall[q, edge:, :] = placed_sum(col_pick, q, lambda w: wide[w])
 
+    def edge_copy(part, device):
+        return links.copy(
+            k_edge[part], wide.at[pl.ds(HB + 2 * part, 2), pl.ds(edge, edge)],
+            edge_in.at[pl.ds(2 * part, 2)], device,
+        )
+
+    def send_edge(part):
+        pl.when((c == 0) & (r < 15))(lambda: edge_copy(part, row_to).start())
+
+    def spread_edge():
+        @pl.when(r > 0)
+        def _():
+            for part in (1, 0):
+                edge_copy(part, row_from).wait_recv()
+            own_pick = {k: v for k, v in col_pick.items() if k[0] >= HB}
+            for q in range(PBD):
+                tall[q, 0:edge, :] = placed_sum(own_pick, q, lambda w: edge_in[w - HB])
+
     def send_rows(span):
-        @pl.when(r < 15)
+        @pl.when((r < 15) & (c > 0))
         def _():
             for made in row_copies(row_to, span):
                 made.start()
@@ -463,7 +483,7 @@
         )
 
     def spread_rows(part):
-        @pl.when(r > 0)
+        @pl.when((r > 0) & (c > 0))
         def _():
             for made in row_copies(row_from, spans[part]):
                 made.wait_recv()
@@ -483,9 +503,11 @@
                 assembled[at] = parent_v[at] + (leave[half * s + k, q] + come[k, q])
 
     update(1)
+    send_edge(1)
     pl.when((c < 15) & ((c > 0) | (yl == 1)))(lambda: col_copy(col_to).start())
     ring.run()
     update(0)
+    send_edge(0)
 
     @pl.when(r == 0)
     def _():
@@ -503,8 +525,8 @@
     def _():
         wide[0:HB] = jnp.zeros((HB,) + wide.shape[1:], F32)
         spread_cols()
-        send_rows(spans[0])
         pl.when(yl == 0)(lambda: col_copy(col_to).start())
+        spread_edge()
         spread_rows(0)
         assemble(0)
         factor = product_nt(halves(assembled[:, :PANEL]), halves(inverse_v[...]))
@@ -560,10 +582,15 @@
     own_sent()
     pl.when(c < 15)(lambda: col_copy(col_to).wait_send())
 
-    @pl.when(r < 15)
+    @pl.when((r < 15) & (c > 0))
     def _():
         for made in row_copies(row_to, (0, PBD)):
             made.wait_send()
+
+    @pl.when((r < 15) & (c == 0))
+    def _():
+        for part in (0, 1):
+            edge_copy(part, row_to).wait_send()
 
     for part in (0, 1):
         sib_copy(part).wait_send()
@@ -594,6 +621,7 @@
             pltpu.VMEM((PANEL, PANEL), F32),
             pltpu.VMEM((CBD + HB, 512, BLK), F32),
             pltpu.VMEM((PBD, 768, BLK), F32),
+            pltpu.VMEM((CBD, 256, BLK), F32),
             pltpu.VMEM((PBD, PBD, BLK, BLK), F32),
             pltpu.VMEM((3, PBD, BLK, BLK), F32),
             pltpu.VMEM((rows, cols), F32),

time: 139 us -> 134 us (0.964)
  the two profiles are of different devices: /device:TPU:17 before, /device:TPU:59 now
where the time goes in v3:
time: 134 us
  Pallas kernels  131 us (98%)
  local copies, waits for them, and re-layouts  2.36 us (2%)
    pallas_call x1, Pallas kernels, shards(): pl.pallas_call(kernel, out_shape=jax.ShapeDtypeStruct(parent.shape, F32),...  131 us

profile of v3, /device:TPU:59, one launch (start us, length us, event | category | flops | bytes accessed | tf_op | source)
XLA Modules:
  0.0 133.5 jit_solution(3969270490091713179)
XLA Ops:
  0.0 131.2 %front_step.1 = f32[384,768]{1,0:T(8,128)} custom-call(f32[1,512,512]{2,1,0:T(8,128)} %front.1, f32[1,32,1024]{2,1,0:T(8,128)} %panel.1, s32[2,64]{1,0:T(2,128)} %block_map.1, f32[384,768]{1,0:T(8,128)} %parent.1, f32[512,512]{1,0:T(8,128)} %inverse.1), custom_call_target="tpu_custom_call" | custom-call | tf_op jit(solution)/shard_map/front_step/pallas_call | solution.py:611
  131.2 2.4 %copy.7 = f32[384,768]{1,0:T(8,128)} copy(f32[384,768]{1,0:T(8,128)} %front_step.1) | data formatting | bytes 2359296
